TPU v7x, 32 devices: a whole 2x2x4 slice. The times are simulated.
32 devices in a mesh: dp: 8 (over y, x, core), branch: 4 (over z).
Axes of the slice: x: 2, y: 2, z: 4, core: 2. Of those that a mesh axis runs over, the one named last changes fastest.
Arguments:
- block_input: bfloat16 [8, 1024, 2048], P('dp', 'branch'), may hold values from -6 to 6
- segment_ids: int32 [8, 1024], P('dp'), may hold values from 0 to 3, as said below
- out_cotangent: bfloat16 [8, 1024, 2048], P('dp', 'branch'), may hold values from -6 to 6
- norm_gain: float32 [2048], replicated, may hold values from 0.5 to 1.5
- norm_bias: float32 [2048], replicated, may hold values from -1.75 to 1.75
- query_weight: bfloat16 [2048, 2048], P('dp', 'branch'), may hold values from -0.125 to 0.125
- key_weight: bfloat16 [2048, 2048], P('dp', 'branch'), may hold values from -0.125 to 0.125
- value_weight: bfloat16 [2048, 2048], P('dp', 'branch'), may hold values from -0.125 to 0.125
- query_bias: float32 [2048], P('branch'), may hold values from -1.75 to 1.75
- key_bias: float32 [2048], P('branch'), may hold values from -1.75 to 1.75
- value_bias: float32 [2048], P('branch'), may hold values from -1.75 to 1.75
- out_weight: bfloat16 [2048, 2048], P('branch', 'dp'), may hold values from -1.5 to 1.5
- fc1_weight: bfloat16 [2048, 8192], P('dp', 'branch'), may hold values from -0.125 to 0.125
- fc1_bias: float32 [8192], P('branch'), may hold values from -3 to 3
- fc2_weight: bfloat16 [8192, 2048], P('branch', 'dp'), may hold values from -0.0625 to 0.0625
- output_bias: float32 [2048], replicated, may hold values from -3 to 3
Outputs:
- block_output: bfloat16 [8, 1024, 2048], P('dp', 'branch')
- input_grad: float32 [8, 1024, 2048], P('dp', 'branch')
- gain_grad: float32 [2048], replicated
- norm_bias_grad: float32 [2048], replicated
- query_weight_grad: float32 [2048, 2048], P('dp', 'branch')
- key_weight_grad: float32 [2048, 2048], P('dp', 'branch')
- value_weight_grad: float32 [2048, 2048], P('dp', 'branch')
- query_bias_grad: float32 [2048], P('branch')
- key_bias_grad: float32 [2048], P('branch')
- value_bias_grad: float32 [2048], P('branch')
- out_weight_grad: float32 [2048, 2048], P('branch', 'dp')
- fc1_weight_grad: float32 [2048, 8192], P('dp', 'branch')
- fc1_bias_grad: float32 [8192], P('branch')
- fc2_weight_grad: float32 [8192, 2048], P('branch', 'dp')
- output_bias_grad: float32 [2048], replicated
Inputs may be any that keep to these rules, and one draw needn't show every extreme that they name: `segment_ids`: in each row of 1024 tokens the values are 1, 2, 3, 0 in runs of that order: documents 1 and 2 (1 may be empty) lie within the first 128 tokens, document 3 begins there and ends within the last 64 tokens, and padding 0 fills the rest, one token or more.
All inputs are finite; a program needn't handle non-finite values.
Results may differ from a plain program's by a relative error of at most 0.012.
The roundings to bfloat16 on the way count: a program that leaves them out, or rounds other values in their place, can miss the bound.
Values may be sent and summed in bfloat16 or wider, within the bound.
A program may use at most 256 MiB of HBM per device.

v0:
```python
import jax
import jax.numpy as jnp
from jax import lax
from jax.sharding import PartitionSpec as P

HEAD_DIM = 64
ROT = 32


EPSILON = 1e-05
NEGATIVE = -1e30


def contract_rows(left, right):
    return lax.dot_general(
        left, right, (((0,), (0,)), ((), ())), preferred_element_type=jnp.float32
    )


def times_transpose(left, right):
    return lax.dot_general(
        left, right, (((1,), (1,)), ((), ())), preferred_element_type=jnp.float32
    )


def rotary_tables(segments):
    row_count, length = segments.shape
    places = jnp.arange(length, dtype=jnp.int32)
    change = jnp.concatenate(
        [jnp.ones((row_count, 1), dtype=jnp.bool_), segments[:, 1:] != segments[:, :-1]], axis=1
    )
    starts = lax.cummax(jnp.where(change, places[None, :], 0), axis=1)
    half_rot = ROT // 2
    frequency = 10000.0 ** (-2.0 * jnp.arange(half_rot, dtype=jnp.float32) / ROT)
    angles = (places[None, :] - starts).astype(jnp.float32)[:, :, None] * frequency
    return (jnp.cos(angles)[:, :, None, :], jnp.sin(angles)[:, :, None, :])


def rotate(tensor, cosine, sine, turn_sign):
    half_rot = ROT // 2
    lower_part = tensor[..., :half_rot]
    upper_part = tensor[..., half_rot:ROT]
    return jnp.concatenate(
        [
            lower_part * cosine - turn_sign * upper_part * sine,
            upper_part * cosine + turn_sign * lower_part * sine,
            tensor[..., ROT:],
        ],
        axis=-1,
    )


def visible(segments, first_row, count):
    length = segments.shape[0]
    query_places = first_row + jnp.arange(count, dtype=jnp.int32)
    key_places = jnp.arange(length, dtype=jnp.int32)
    query_segments = lax.dynamic_slice_in_dim(segments, first_row, count)
    same_doc = query_segments[:, None] == segments[None, :]
    causal = key_places[None, :] <= query_places[:, None]
    live_key = segments[None, :] != 0
    return same_doc & causal & live_key | (key_places[None, :] == query_places[:, None])


def block_scores(query_block, keys, segments, first_row):
    scores = jnp.einsum(
        "qhd,khd->hqk", query_block, keys, preferred_element_type=jnp.float32
    ) * HEAD_DIM ** (-0.5)
    return jnp.where(visible(segments, first_row, query_block.shape[0])[None], scores, NEGATIVE)


def attend_row(queries, keys, values, segments):
    length = queries.shape[0]
    block_rows = min(512, length)

    def one_block(block_index):
        first_row = block_index * block_rows
        query_block = lax.dynamic_slice_in_dim(queries, first_row, block_rows, 0)
        scores = block_scores(query_block, keys, segments, first_row)
        row_max = jnp.max(scores, axis=-1, keepdims=True)
        exponent = jnp.exp(scores - row_max)
        totals = jnp.sum(exponent, axis=-1, keepdims=True)
        probability = (exponent / totals).astype(jnp.bfloat16)
        block_out = jnp.einsum(
            "hqk,khd->qhd", probability, values, preferred_element_type=jnp.float32
        )
        return (block_out, row_max, totals)

    outputs, maxima, row_sums = lax.map(
        one_block, jnp.arange(length // block_rows, dtype=jnp.int32)
    )
    return (outputs.reshape(queries.shape), maxima, row_sums)


def attend_row_back(queries, keys, values, out_grad, maxima, row_sums, segments):
    length = queries.shape[0]
    block_rows = min(512, length)
    scale = HEAD_DIM ** (-0.5)

    def one_block(carry, block_index):
        key_grad, value_grad = carry
        first_row = block_index * block_rows
        query_block = lax.dynamic_slice_in_dim(queries, first_row, block_rows, 0)
        grad_block = lax.dynamic_slice_in_dim(out_grad, first_row, block_rows, 0)
        scores = block_scores(query_block, keys, segments, first_row)
        probability = jnp.exp(scores - maxima[block_index]) / row_sums[block_index]
        prob_low = probability.astype(jnp.bfloat16)
        prob_grad = jnp.einsum(
            "qhd,khd->hqk", grad_block, values, preferred_element_type=jnp.float32
        )
        delta = jnp.sum(probability * prob_grad, axis=-1, keepdims=True)
        score_grad = (probability * (prob_grad - delta)).astype(jnp.bfloat16)
        query_grad = (
            jnp.einsum("hqk,khd->qhd", score_grad, keys, preferred_element_type=jnp.float32) * scale
        )
        key_grad = (
            key_grad
            + jnp.einsum(
                "hqk,qhd->khd", score_grad, query_block, preferred_element_type=jnp.float32
            )
            * scale
        )
        value_grad = value_grad + jnp.einsum(
            "hqk,qhd->khd", prob_low, grad_block, preferred_element_type=jnp.float32
        )
        return ((key_grad, value_grad), query_grad)

    zeros = jnp.zeros(keys.shape, jnp.float32)
    (key_grad, value_grad), query_grads = lax.scan(
        one_block, (zeros, zeros), jnp.arange(length // block_rows, dtype=jnp.int32)
    )
    return (query_grads.reshape(queries.shape), key_grad, value_grad)


def on_device(
    block_input,
    segment_ids,
    out_cotangent,
    norm_gain,
    norm_bias,
    query_weight,
    key_weight,
    value_weight,
    query_bias,
    key_bias,
    value_bias,
    out_weight,
    fc1_weight,
    fc1_bias,
    fc2_weight,
    output_bias,
):
    row_count = block_input.shape[0]
    width = block_input.shape[2]
    inputs = block_input.astype(jnp.float32)
    center = inputs - jnp.mean(inputs, axis=-1, keepdims=True)
    inverse = lax.rsqrt(jnp.mean(center * center, axis=-1, keepdims=True) + EPSILON)
    normed = center * inverse
    shard_hidden = (normed * norm_gain + norm_bias).astype(jnp.bfloat16)
    hidden = lax.all_gather(shard_hidden, "branch", axis=1, tiled=True)
    length = hidden.shape[1]
    tokens = row_count * length
    flat_hidden = hidden.reshape(tokens, width)
    gathered = (
        lax.all_gather(query_weight, "dp", axis=0, tiled=True),
        lax.all_gather(key_weight, "dp", axis=0, tiled=True),
        lax.all_gather(value_weight, "dp", axis=0, tiled=True),
        lax.all_gather(fc1_weight, "dp", axis=0, tiled=True),
        lax.all_gather(out_weight, "dp", axis=1, tiled=True),
        lax.all_gather(fc2_weight, "dp", axis=1, tiled=True),
    )
    full_query, full_key, full_value, full_fc1, full_out, full_fc2 = gathered
    heads_local = full_query.shape[1] // HEAD_DIM
    cosine, sine = rotary_tables(segment_ids)
    head_shape = (row_count, length, heads_local, HEAD_DIM)
    query_raw = (
        jnp.dot(flat_hidden, full_query, preferred_element_type=jnp.float32) + query_bias
    ).reshape(head_shape)
    key_raw = (
        jnp.dot(flat_hidden, full_key, preferred_element_type=jnp.float32) + key_bias
    ).reshape(head_shape)
    query_rot = rotate(query_raw, cosine, sine, 1.0).astype(jnp.bfloat16)
    key_rot = rotate(key_raw, cosine, sine, 1.0).astype(jnp.bfloat16)
    value_low = (
        (jnp.dot(flat_hidden, full_value, preferred_element_type=jnp.float32) + value_bias)
        .astype(jnp.bfloat16)
        .reshape(head_shape)
    )
    attended, maxima, row_sums = lax.map(
        lambda member: attend_row(*member), (query_rot, key_rot, value_low, segment_ids)
    )
    attended = attended.astype(jnp.bfloat16).reshape(tokens, heads_local * HEAD_DIM)
    pre_act = jnp.dot(flat_hidden, full_fc1, preferred_element_type=jnp.float32) + fc1_bias
    activation = jax.nn.gelu(pre_act, approximate=True).astype(jnp.bfloat16)
    partial_value = jnp.dot(attended, full_out, preferred_element_type=jnp.float32) + jnp.dot(
        activation, full_fc2, preferred_element_type=jnp.float32
    )
    summed = lax.psum_scatter(
        partial_value.reshape(row_count, length, width), "branch", scatter_dimension=1, tiled=True
    )
    block_output = (inputs + summed + output_bias).astype(jnp.bfloat16)
    cot_full = lax.all_gather(out_cotangent, "branch", axis=1, tiled=True).reshape(tokens, width)
    back_set = (
        lax.all_gather(query_weight, "dp", axis=0, tiled=True),
        lax.all_gather(key_weight, "dp", axis=0, tiled=True),
        lax.all_gather(value_weight, "dp", axis=0, tiled=True),
        lax.all_gather(fc1_weight, "dp", axis=0, tiled=True),
        lax.all_gather(out_weight, "dp", axis=1, tiled=True),
        lax.all_gather(fc2_weight, "dp", axis=1, tiled=True),
    )
    back_query, back_key, back_value, back_fc1, back_out, back_fc2 = back_set
    output_bias_grad = jnp.sum(cot_full, axis=0, dtype=jnp.float32)
    out_weight_grad = contract_rows(attended, cot_full)
    fc2_weight_grad = contract_rows(activation, cot_full)
    act_grad = times_transpose(cot_full, back_fc2)
    _, gelu_pull = jax.vjp(lambda inner: jax.nn.gelu(inner, approximate=True), pre_act)
    pre_grad = gelu_pull(act_grad)[0].astype(jnp.bfloat16)
    fc1_weight_grad = contract_rows(flat_hidden, pre_grad)
    fc1_bias_grad = jnp.sum(pre_grad, axis=0, dtype=jnp.float32)
    hidden_grad = times_transpose(pre_grad, back_fc1)
    att_grad = times_transpose(cot_full, back_out).astype(jnp.bfloat16).reshape(head_shape)
    dquery, dkey, dvalue = lax.map(
        lambda member: attend_row_back(*member),
        (query_rot, key_rot, value_low, att_grad, maxima, row_sums, segment_ids),
    )
    query_grad = (
        rotate(dquery, cosine, sine, -1.0)
        .astype(jnp.bfloat16)
        .reshape(tokens, heads_local * HEAD_DIM)
    )
    key_grad = (
        rotate(dkey, cosine, sine, -1.0)
        .astype(jnp.bfloat16)
        .reshape(tokens, heads_local * HEAD_DIM)
    )
    value_grad = dvalue.astype(jnp.bfloat16).reshape(tokens, heads_local * HEAD_DIM)
    query_weight_grad = contract_rows(flat_hidden, query_grad)
    key_weight_grad = contract_rows(flat_hidden, key_grad)
    value_weight_grad = contract_rows(flat_hidden, value_grad)
    query_bias_grad = jnp.sum(query_grad, axis=0, dtype=jnp.float32)
    key_bias_grad = jnp.sum(key_grad, axis=0, dtype=jnp.float32)
    value_bias_grad = jnp.sum(value_grad, axis=0, dtype=jnp.float32)
    hidden_grad = (
        hidden_grad
        + times_transpose(query_grad, back_query)
        + times_transpose(key_grad, back_key)
        + times_transpose(value_grad, back_value)
    )
    norm_grad = lax.psum_scatter(
        hidden_grad.reshape(row_count, length, width), "branch", scatter_dimension=1, tiled=True
    )
    gain_part = jnp.sum(norm_grad * normed, axis=(0, 1))
    beta_part = jnp.sum(norm_grad, axis=(0, 1))
    scaled = norm_grad * norm_gain
    input_grad = out_cotangent.astype(jnp.float32) + inverse * (
        scaled
        - jnp.mean(scaled, axis=-1, keepdims=True)
        - normed * jnp.mean(scaled * normed, axis=-1, keepdims=True)
    )
    gain_grad, norm_bias_grad = lax.psum((gain_part, beta_part), ("dp", "branch"))
    query_bias_grad, key_bias_grad, value_bias_grad, fc1_bias_grad, output_bias_grad = lax.psum(
        (query_bias_grad, key_bias_grad, value_bias_grad, fc1_bias_grad, output_bias_grad), "dp"
    )
    (
        query_weight_grad,
        key_weight_grad,
        value_weight_grad,
        fc1_weight_grad,
        out_weight_grad,
        fc2_weight_grad,
    ) = (
        lax.psum_scatter(query_weight_grad, "dp", scatter_dimension=0, tiled=True),
        lax.psum_scatter(key_weight_grad, "dp", scatter_dimension=0, tiled=True),
        lax.psum_scatter(value_weight_grad, "dp", scatter_dimension=0, tiled=True),
        lax.psum_scatter(fc1_weight_grad, "dp", scatter_dimension=0, tiled=True),
        lax.psum_scatter(out_weight_grad, "dp", scatter_dimension=1, tiled=True),
        lax.psum_scatter(fc2_weight_grad, "dp", scatter_dimension=1, tiled=True),
    )
    return (
        block_output,
        input_grad,
        gain_grad,
        norm_bias_grad,
        query_weight_grad,
        key_weight_grad,
        value_weight_grad,
        query_bias_grad,
        key_bias_grad,
        value_bias_grad,
        out_weight_grad,
        fc1_weight_grad,
        fc1_bias_grad,
        fc2_weight_grad,
        output_bias_grad,
    )


def solution(mesh):
    in_specs = (
        P("dp", "branch", None),
        P("dp", None),
        P("dp", "branch", None),
        P(),
        P(),
        P("dp", "branch"),
        P("dp", "branch"),
        P("dp", "branch"),
        P("branch"),
        P("branch"),
        P("branch"),
        P("branch", "dp"),
        P("dp", "branch"),
        P("branch"),
        P("branch", "dp"),
        P(),
    )
    out_specs = (
        P("dp", "branch", None),
        P("dp", "branch", None),
        P(),
        P(),
        P("dp", "branch"),
        P("dp", "branch"),
        P("dp", "branch"),
        P("branch"),
        P("branch"),
        P("branch"),
        P("branch", "dp"),
        P("dp", "branch"),
        P("branch"),
        P("branch", "dp"),
        P(),
    )
    return jax.shard_map(
        on_device, mesh=mesh, in_specs=in_specs, out_specs=out_specs, check_vma=False
    )
```

profile of v0, /device:TPU:0, one launch (start us, length us, event | category | flops | bytes accessed | tf_op | source)
XLA Modules:
  0.0 1306.7 jit_solution(10500603375588209174)
XLA Ops:
  9.4 1.6 fusion.76
  11.7 2.7 fusion.70
  20.4 20.2 %all-gather.11.cloned.1.call-done = bf16[2048,512]{1,0:T(8,128)(2,1)} async-done(((bf16[256,512]{1,0:T(8,128)(2,1)}), bf16[2048,512]{1,0:T(8,128)(2,1)}) %all-gather.11.cloned.1.call-update) | async-done | bytes 2097168 | tf_op jit(solution)/shard_map/all_gather | solution.py:164
  40.5 82.9 %all-gather.9.cloned.1.call-done = bf16[1,1024,2048]{2,1,0:T(8,128)(2,1)} async-done(((bf16[1,256,2048]{2,1,0:T(8,128)(2,1)}), bf16[1,1024,2048]{2,1,0:T(8,128)(2,1)}) %all-gather.9.cloned.1.call-update) | async-done | bytes 4194320 | tf_op jit(solution)/shard_map/all_gather | solution.py:159
  123.5 5.2 fusion.79
  130.1 21.7 %all-gather.13.cloned.1.call-done = bf16[2048,512]{1,0:T(8,128)(2,1)} async-done(((bf16[256,512]{1,0:T(8,128)(2,1)}), bf16[2048,512]{1,0:T(8,128)(2,1)}) %all-gather.13.cloned.1.call-update) | async-done | bytes 2097168 | tf_op jit(solution)/shard_map/all_gather | solution.py:165
  151.8 5.4 fusion.82
  158.8 22.6 %all-gather.15.cloned.1.call-done = bf16[2048,512]{1,0:T(8,128)(2,1)} async-done(((bf16[256,512]{1,0:T(8,128)(2,1)}), bf16[2048,512]{1,0:T(8,128)(2,1)}) %all-gather.15.cloned.1.call-update) | async-done | bytes 2097168 | tf_op jit(solution)/shard_map/all_gather | solution.py:166
  181.5 6.2 add_convert_fusion
  187.7 34.8 %while.51 = (s32[]{:T(128)}, bf16[2,512,8,64]{1,3,2,0:T(8,128)(2,1)}, f32[2,8,512,1]{2,1,3,0:T(8,128)S(1)}, f32[2,8,512,1]{2,1,3,0:T(8,128)S(1)}, s32[2]{0:T(128...) while((s32[]{:T(128)}, ...), condition=%wide.region_7.8_spmd, body=%wide.region_4.7_spmd.sunk | while | flops 1127212544 | bytes 56266960 | solution.py:88
  190.4 4.1 fusion.152
  194.5 4.2 fusion.153
  198.8 6.6 fusion.154
  207.6 4.1 fusion.152
  211.7 4.2 fusion.153
  215.9 6.7 fusion.154
  222.6 71.0 %all-gather.23.cloned.1.call-done = bf16[1,1024,2048]{2,1,0:T(8,128)(2,1)} async-done(((bf16[1,256,2048]{2,1,0:T(8,128)(2,1)}), bf16[1,1024,2048]{2,1,0:T(8,128)(2,1)}) %all-gather.23.cloned.1.call-update) | async-done | bytes 4194320 | tf_op jit(solution)/shard_map/all_gather | solution.py:201
  293.7 6.2 fusion.87
  299.9 163.0 %while.52 = (s32[]{:T(128)}, f32[1024,8,64]{0,2,1:T(8,128)S(1)}, f32[1024,8,64]{0,2,1:T(8,128)}, f32[2,512,8,64]{1,0,3,2:T(2,128)}, s32[2]{0:T(128)S(1)}, /*inde...) while((s32[]{:T(128)}, f32[1024,8,64]{0,2,1:T(8,128)S(1)}, ...), condition=%wide.region_11.12_spmd.clone, body=%wide.region_9.11_spmd.clone.sunk | while | flops 2732324352 | bytes 192041392 | solution.py:128
  301.3 9.7 fusion.164
  313.9 13.7 %multiply_reduce_fusion.3 = (f32[8,512]{1,0:T(8,128)S(1)}, f32[8,512,1024]{2,1,0:T(8,128)}) fusion(f32[8,512,1024]{2,1,0:T(8,128)} %fusion.164, f32[8,512]{1,0:T(8,128)S(1)} %get-tuple-element.458, f32[8,512]{1,0:T(8,128)S(1)} %get-tuple-element.459, bf16[1024,8,64]{0,2,1:T(8,128)(2,1)S(1)} %get-tuple-element.542, ...), kind=kOutput, calls=%fused_computation.23.clone.1 | convolution fusion | flops 562032640 | bytes 35700740 | tf_op jit(solution)/shard_map/while/body/eval_jaxpr/while/body/eval_jaxpr/qhd,khd->hqk/dot_general | solution.py:65
  327.6 15.2 %multiply_convert_fusion.5 = bf16[8,512,1024]{2,1,0:T(8,128)(2,1)} fusion(f32[8,512,1024]{2,1,0:T(8,128)} %get-tuple-element.460, f32[8,512,1024]{2,1,0:T(8,128)} %fusion.164, f32[8,512]{1,0:T(8,128)S(1)} %get-tuple-element.461), kind=kLoop, calls=%fused_computation.22.clone.1 | loop fusion | flops 12582912 | bytes 41959424 | tf_op jit(solution)/shard_map/while/body/eval_jaxpr/while/body/eval_jaxpr/convert_element_type | solution.py:111
  342.8 5.5 bitcast_add_fusion.4
  348.3 7.8 bitcast_add_fusion.5
  357.4 2.7 fusion.166
  360.1 2.1 copy.48
  362.1 19.7 %dynamic_update_slice.37 = f32[2,512,8,64]{1,0,3,2:T(2,128)} dynamic-update-slice(f32[2,512,8,64]{1,0,3,2:T(2,128)} %get-tuple-element.521, f32[1,512,8,64]{1,0,3,2:T(1,128)} %copy.48, s32[]{:T(128)S(6)} %copy.69, s32[]{:T(128)} %constant.94.clone.1..sunk.1, s32[]{:T(128)} %constant.94.clone.1..sunk.1, s32[]{:T(128)} %constant.94.clone.1..sunk.1) | dynamic-update-slice | bytes 2097156 | tf_op jit(solution)/shard_map/while/body/eval_jaxpr/while/body/jit(dynamic_update_index_in_dim)/dynamic_update_slice | solution.py:88
  383.1 9.5 fusion.164
  395.5 13.3 %multiply_reduce_fusion.3 = (f32[8,512]{1,0:T(8,128)S(1)}, f32[8,512,1024]{2,1,0:T(8,128)}) fusion(f32[8,512,1024]{2,1,0:T(8,128)} %fusion.164, f32[8,512]{1,0:T(8,128)S(1)} %get-tuple-element.458, f32[8,512]{1,0:T(8,128)S(1)} %get-tuple-element.459, bf16[1024,8,64]{0,2,1:T(8,128)(2,1)S(1)} %get-tuple-element.542, ...), kind=kOutput, calls=%fused_computation.23.clone.1 | convolution fusion | flops 562032640 | bytes 35700740 | tf_op jit(solution)/shard_map/while/body/eval_jaxpr/while/body/eval_jaxpr/qhd,khd->hqk/dot_general | solution.py:65
  408.8 14.9 %multiply_convert_fusion.5 = bf16[8,512,1024]{2,1,0:T(8,128)(2,1)} fusion(f32[8,512,1024]{2,1,0:T(8,128)} %get-tuple-element.460, f32[8,512,1024]{2,1,0:T(8,128)} %fusion.164, f32[8,512]{1,0:T(8,128)S(1)} %get-tuple-element.461), kind=kLoop, calls=%fused_computation.22.clone.1 | loop fusion | flops 12582912 | bytes 41959424 | tf_op jit(solution)/shard_map/while/body/eval_jaxpr/while/body/eval_jaxpr/convert_element_type | solution.py:111
  423.6 5.5 bitcast_add_fusion.4
  429.1 7.8 bitcast_add_fusion.5
  438.3 2.7 fusion.166
  441.0 2.1 copy.48
  443.0 19.6 %dynamic_update_slice.37 = f32[2,512,8,64]{1,0,3,2:T(2,128)} dynamic-update-slice(f32[2,512,8,64]{1,0,3,2:T(2,128)} %get-tuple-element.521, f32[1,512,8,64]{1,0,3,2:T(1,128)} %copy.48, s32[]{:T(128)S(6)} %copy.69, s32[]{:T(128)} %constant.94.clone.1..sunk.1, s32[]{:T(128)} %constant.94.clone.1..sunk.1, s32[]{:T(128)} %constant.94.clone.1..sunk.1) | dynamic-update-slice | bytes 2097156 | tf_op jit(solution)/shard_map/while/body/eval_jaxpr/while/body/jit(dynamic_update_index_in_dim)/dynamic_update_slice | solution.py:88
  463.0 4.0 broadcast_in_dim.94
  472.5 5.6 fusion.101
  478.1 5.6 fusion.100
  483.8 14.4 %fusion.53 = f32[1024,2048]{1,0:T(8,128)} fusion(bf16[2048,2048]{1,0:T(8,128)(2,1)} %all-gather.19.cloned.1.call-done, bf16[1,1024,2048]{2,1,0:T(8,128)(2,1)} %all-gather.9.cloned.1.call-done), kind=kOutput, calls=%fused_computation.79 | convolution fusion | flops 8589934592 | bytes 20971520 | tf_op jit(solution)/shard_map/dot_general | solution.py:192
  498.2 20.3 %convert_reduce_fusion.1 = (f32[2048]{0:T(1024)S(1)}, bf16[1024,2048]{1,0:T(8,128)(2,1)}) fusion(f32[1024,2048]{1,0:T(8,128)} %fusion.53, f32[2048]{0:T(1024)S(1)} %copy-done.27, bf16[2048,2048]{1,0:T(8,128)(2,1)} %all-gather.21.cloned.1.call-done, bf16[1,1024,2048]{2,1,0:T(8,128)(2,1)} %all-gather.23.cloned.1.call-done), kind=kOutput, calls=%fused_computation.59 | convolution fusion | flops 8638167040 | bytes 25182208 | tf_op jit(solution)/shard_map/dot_general | solution.py:21
  518.5 14.8 %fusion.99 = f32[1024,2048]{1,0:T(8,128)} fusion(bf16[1024,2048]{1,0:T(8,128)(2,1)} %get-tuple-element.315, bf16[2048,2048]{1,0:T(8,128)(2,1)} %all-gather.19.cloned.1.call-done), kind=kOutput, calls=%fused_computation.151 | convolution fusion | flops 8589934592 | bytes 20971520 | tf_op jit(solution)/shard_map/dot_general | solution.py:21
  533.4 12.0 add_bitcast_fusion
  545.5 2.3 copy.31
  548.0 16.4 %fusion.98 = f32[1024,2048]{1,0:T(8,128)S(1)} fusion(bf16[2048,2048]{1,0:T(8,128)(2,1)} %all-gather.21.cloned.1.call-done, f32[1024,2048]{1,0:T(8,128)} %fusion.53, f32[2048]{0:T(1024)S(1)} %copy-done.27), kind=kOutput, calls=%fused_computation.150 | convolution fusion | flops 8610906112 | bytes 25174016 | tf_op jit(solution)/shard_map/dot_general | solution.py:194
  564.4 5.6 add_bitcast_fusion.1
  570.4 6.9 fusion.51
  577.3 6.5 fusion.49
  583.9 6.7 fusion.47
  590.7 6.5 fusion.39
  597.5 15.2 %fusion.45 = f32[2048,2048]{1,0:T(8,128)} fusion(bf16[1024,2048]{1,0:T(8,128)(2,1)} %get-tuple-element.315, bf16[1,1024,2048]{2,1,0:T(8,128)(2,1)} %all-gather.9.cloned.1.call-done), kind=kOutput, calls=%fused_computation.71 | convolution fusion | flops 8589934592 | bytes 25165824 | tf_op jit(solution)/shard_map/dot_general | solution.py:15
  612.8 17.3 %fusion.37 = f32[2048,2048]{1,0:T(8,128)} fusion(bf16[1,1024,2048]{2,1,0:T(8,128)(2,1)} %all-gather.23.cloned.1.call-done, f32[1024,2048]{1,0:T(8,128)} %fusion.53, f32[2048]{0:T(1024)S(1)} %copy-done.27), kind=kOutput, calls=%fused_computation.63 | convolution fusion | flops 8610906112 | bytes 29368320 | tf_op jit(solution)/shard_map/dot_general | solution.py:15
  631.0 2.9 convert_reduce_fusion
  633.8 24.7 %all-reduce.1 = (f32[512]{0:T(512)}, f32[512]{0:T(512)}, f32[512]{0:T(512)}, f32[2048]{0:T(1024)}, f32[2048]{0:T(1024)}) all-reduce(f32[512]{0:T(512)S(1)} %reduce_sum.130, f32[512]{0:T(512)S(1)} %reduce_sum.132, f32[512]{0:T(512)S(1)} %reduce_sum.134, f32[2048]{0:T(1024)S(1)} %get-tuple-element.314, ...), channel_id=1, replica_groups=mesh['dp'=8,'branch'=4] {'dp'}, use_global_device_ids=true, to_apply=%region_23.24 | all-reduce | flops 5632 | bytes 45056 | tf_op jit(solution)/shard_map/psum | solution.py:260
  658.6 30.5 %reduce-scatter.11.cloned.1.call-done = f32[1,256,2048]{2,1,0:T(8,128)} async-done(((f32[1,1024,2048]{2,1,0:T(8,128)}), f32[1,256,2048]{2,1,0:T(8,128)}) %reduce-scatter.11.cloned.1.call-update) | async-done | bytes 2097168 | tf_op jit(solution)/shard_map/reduce_scatter | solution.py:248
  689.0 2.7 fusion.75
  691.8 45.9 %all-reduce = (f32[2048]{0:T(1024)}, f32[2048]{0:T(1024)}) all-reduce(f32[2048]{0:T(1024)S(1)} %get-tuple-element.230, f32[2048]{0:T(1024)S(1)} %get-tuple-element.233), channel_id=1, replica_groups=mesh['dp'=8,'branch'=4] {'dp','branch'}, use_global_device_ids=true, to_apply=%region_16.17 | all-reduce | flops 4096 | bytes 32768 | tf_op jit(solution)/shard_map/psum | solution.py:259
  737.7 99.7 %reduce-scatter.9.cloned.1.call-done = f32[1,256,2048]{2,1,0:T(8,128)} async-done(((f32[1,1024,2048]{2,1,0:T(8,128)}), f32[1,256,2048]{2,1,0:T(8,128)}) %reduce-scatter.9.cloned.1.call-update) | async-done | bytes 2097168 | tf_op jit(solution)/shard_map/reduce_scatter | solution.py:197
  837.4 4.7 fusion.74
  842.0 51.4 %reduce-scatter.13.cloned.1.call-done = f32[256,512]{1,0:T(8,128)} async-done(((f32[2048,512]{1,0:T(8,128)}), f32[256,512]{1,0:T(8,128)}) %reduce-scatter.13.cloned.1.call-update) | async-done | bytes 524304 | tf_op jit(solution)/shard_map/reduce_scatter | solution.py:271
  893.5 55.5 %reduce-scatter.15.cloned.1.call-done = f32[256,512]{1,0:T(8,128)} async-done(((f32[2048,512]{1,0:T(8,128)}), f32[256,512]{1,0:T(8,128)}) %reduce-scatter.15.cloned.1.call-update) | async-done | bytes 524304 | tf_op jit(solution)/shard_map/reduce_scatter | solution.py:272
  949.0 55.3 %reduce-scatter.17.cloned.1.call-done = f32[256,512]{1,0:T(8,128)} async-done(((f32[2048,512]{1,0:T(8,128)}), f32[256,512]{1,0:T(8,128)}) %reduce-scatter.17.cloned.1.call-update) | async-done | bytes 524304 | tf_op jit(solution)/shard_map/reduce_scatter | solution.py:273
  1004.3 55.5 %reduce-scatter.19.cloned.1.call-done = f32[512,256]{1,0:T(8,128)} async-done(((f32[512,2048]{1,0:T(8,128)}), f32[512,256]{1,0:T(8,128)}) %reduce-scatter.19.cloned.1.call-update) | async-done | bytes 524304 | tf_op jit(solution)/shard_map/reduce_scatter | solution.py:275
  1059.8 120.0 %reduce-scatter.21.cloned.1.call-done = f32[256,2048]{1,0:T(8,128)} async-done(((f32[2048,2048]{1,0:T(8,128)}), f32[256,2048]{1,0:T(8,128)}) %reduce-scatter.21.cloned.1.call-update) | async-done | bytes 2097168 | tf_op jit(solution)/shard_map/reduce_scatter | solution.py:274
  1179.8 120.0 %reduce-scatter.23.cloned.1.call-done = f32[2048,256]{1,0:T(8,128)} async-done(((f32[2048,2048]{1,0:T(8,128)}), f32[2048,256]{1,0:T(8,128)}) %reduce-scatter.23.cloned.1.call-update) | async-done | bytes 2097168 | tf_op jit(solution)/shard_map/reduce_scatter | solution.py:276
  (180 shorter events, 28.1 us)
Async XLA Ops:
  7.2 33.4 %all-gather.11.cloned.1.call-start = ((), (), s32[]{:S(2)}) async-start(), calls=%async_computation.9 | async-start | bytes 2359296 | tf_op jit(solution)/shard_map/all_gather | solution.py:164
  7.9 115.6 %all-gather.9.cloned.1.call-start = ((), (), s32[]{:S(2)}) async-start(), calls=%async_computation.8 | async-start | bytes 5242880 | tf_op jit(solution)/shard_map/all_gather | solution.py:159
  9.4 9.1 copy-start.7
  9.4 1.7 copy-start.17
  9.4 114.0 %copy-start.28 = (f32[512]{0:T(512)S(1)}, f32[512]{0:T(512)}, u32[]{:S(2)}) copy-start(f32[512]{0:T(512)} %param.28) | copy-start | bytes 6148
  11.1 0.6 copy-start.19
  14.4 137.4 %all-gather.13.cloned.1.call-start = ((), (), s32[]{:S(2)}) async-start(), calls=%async_computation.10 | async-start | bytes 2359296 | tf_op jit(solution)/shard_map/all_gather | solution.py:165
  15.1 166.4 %all-gather.15.cloned.1.call-start = ((), (), s32[]{:S(2)}) async-start(), calls=%async_computation.11 | async-start | bytes 2359296 | tf_op jit(solution)/shard_map/all_gather | solution.py:166
  15.7 206.9 %all-gather.17.cloned.1.call-start = ((), (), s32[]{:S(2)}) async-start(), calls=%async_computation.12 | async-start | bytes 2359296 | tf_op jit(solution)/shard_map/all_gather | solution.py:168
  16.3 277.4 %all-gather.23.cloned.1.call-start = ((), (), s32[]{:S(2)}) async-start(), calls=%async_computation.16 | async-start | bytes 5242880 | tf_op jit(solution)/shard_map/all_gather | solution.py:201
  16.9 466.9 %all-gather.19.cloned.1.call-start = ((), (), s32[]{:S(2)}) async-start(), calls=%async_computation.13 | async-start | bytes 9437184 | tf_op jit(solution)/shard_map/all_gather | solution.py:167
  17.6 480.6 %all-gather.21.cloned.1.call-start = ((), (), s32[]{:S(2)}) async-start(), calls=%async_computation.14 | async-start | bytes 9437184 | tf_op jit(solution)/shard_map/all_gather | solution.py:169
  18.3 670.7 %reduce-scatter.11.cloned.1.call-start = ((), (), s32[]{:S(2)}) async-start(), calls=%async_computation.17 | async-start | bytes 10485760 | tf_op jit(solution)/shard_map/reduce_scatter | solution.py:248
  20.4 136.9 %copy-start.13 = (f32[1024,16]{0,1:T(8,128)}, f32[1024,16]{0,1:T(8,128)S(1)}, u32[]{:S(2)}) copy-start(f32[1024,16]{0,1:T(8,128)S(1)} %get-tuple-element.313) | copy-start | bytes 196612
  20.4 131.5 %copy-start.29 = (f32[512]{0:T(512)S(1)}, f32[512]{0:T(512)}, u32[]{:S(2)}) copy-start(f32[512]{0:T(512)} %param.29) | copy-start | bytes 6148
  128.7 1.3 copy-start.10
  151.8 5.5 copy-start.11
  157.2 24.3 %copy-start.30 = (f32[512]{0:T(512)S(1)}, f32[512]{0:T(512)}, u32[]{:S(2)}) copy-start(f32[512]{0:T(512)} %param.30) | copy-start | bytes 6148
  222.6 77.3 %copy-start = (f32[1024,8,64]{0,2,1:T(8,128)S(1)}, f32[1024,8,64]{0,2,1:T(8,128)}, u32[]{:S(2)}) copy-start(f32[1024,8,64]{0,2,1:T(8,128)} %custom-call) | copy-start | bytes 6291460
  342.8 5.5 copy-start.1
  342.8 5.5 copy-start.4
  342.8 14.6 %slice-start = ((s8[8388608]{0:T(1024)(128)(4,1)}), s8[4194304]{0:T(1024)(128)(4,1)S(1)}, s32[]{:S(2)}) async-start(s8[8388608]{0:T(1024)(128)(4,1)} %bitcast.166), calls=%async_computation.24 | async-start | bytes 8388608 | tf_op jit(solution)/shard_map/while/body/eval_jaxpr/while
  348.3 9.1 slice-start.1
  356.1 1.3 copy-start.2
  423.6 5.5 copy-start.1
  423.6 5.5 copy-start.4
  423.6 14.7 %slice-start = ((s8[8388608]{0:T(1024)(128)(4,1)}), s8[4194304]{0:T(1024)(128)(4,1)S(1)}, s32[]{:S(2)}) async-start(s8[8388608]{0:T(1024)(128)(4,1)} %bitcast.166), calls=%async_computation.24 | async-start | bytes 8388608 | tf_op jit(solution)/shard_map/while/body/eval_jaxpr/while
  429.1 9.2 slice-start.1
  437.0 1.3 copy-start.2
  462.9 5.6 copy-start.14
  462.9 5.6 copy-start.15
  467.0 4.6 copy-start.3
  469.9 2.6 copy-start.26
  471.6 6.6 copy-start.12
  472.5 5.6 copy-start.25
  483.8 14.4 %copy-start.27 = (f32[2048]{0:T(1024)S(1)}, f32[2048]{0:T(1024)}, u32[]{:S(2)}) copy-start(f32[2048]{0:T(1024)} %param.33) | copy-start | bytes 24580
  518.5 14.8 %slice-start.2 = ((s8[8388608]{0:T(1024)(128)(4,1)}), s8[4194304]{0:T(1024)(128)(4,1)S(1)}, s32[]{:S(2)}) async-start(s8[8388608]{0:T(1024)(128)(4,1)} %bitcast.171), calls=%async_computation.26 | async-start | bytes 8388608
  518.5 14.8 %slice-start.3 = ((s8[8388608]{0:T(1024)(128)(4,1)}), s8[4194304]{0:T(1024)(128)(4,1)S(1)}, s32[]{:S(2)}) async-start(s8[8388608]{0:T(1024)(128)(4,1)} %bitcast.171), calls=%async_computation.27 | async-start | bytes 8388608
  518.5 14.8 %copy-start.9 = (bf16[2048,512]{1,0:T(8,128)(2,1)S(1)}, bf16[2048,512]{1,0:T(8,128)(2,1)}, u32[]{:S(2)}) copy-start(bf16[2048,512]{1,0:T(8,128)(2,1)} %all-gather.15.cloned.1.call-done) | copy-start | bytes 6291460
  545.4 291.9 %reduce-scatter.9.cloned.1.call-start = ((), (), s32[]{:S(2)}) async-start(), calls=%async_computation.15 | async-start | bytes 10485760 | tf_op jit(solution)/shard_map/reduce_scatter | solution.py:197
  548.0 16.4 %copy-start.8 = (bf16[512,2048]{1,0:T(8,128)(2,1)S(1)}, bf16[512,2048]{1,0:T(8,128)(2,1)}, u32[]{:S(2)}) copy-start(bf16[512,2048]{1,0:T(8,128)(2,1)} %all-gather.17.cloned.1.call-done) | copy-start | bytes 6291460
  570.1 323.4 %reduce-scatter.13.cloned.1.call-start = ((), (), s32[]{:S(2)}) async-start(), calls=%async_computation.18 | async-start | bytes 4718592 | tf_op jit(solution)/shard_map/reduce_scatter | solution.py:271
  577.3 371.7 %reduce-scatter.15.cloned.1.call-start = ((), (), s32[]{:S(2)}) async-start(), calls=%async_computation.19 | async-start | bytes 4718592 | tf_op jit(solution)/shard_map/reduce_scatter | solution.py:272
  583.9 420.4 %reduce-scatter.17.cloned.1.call-start = ((), (), s32[]{:S(2)}) async-start(), calls=%async_computation.20 | async-start | bytes 4718592 | tf_op jit(solution)/shard_map/reduce_scatter | solution.py:273
  590.6 469.1 %reduce-scatter.19.cloned.1.call-start = ((), (), s32[]{:S(2)}) async-start(), calls=%async_computation.21 | async-start | bytes 4718592 | tf_op jit(solution)/shard_map/reduce_scatter | solution.py:275
  597.2 582.5 %reduce-scatter.21.cloned.1.call-start = ((), (), s32[]{:S(2)}) async-start(), calls=%async_computation.22 | async-start | bytes 18874368 | tf_op jit(solution)/shard_map/reduce_scatter | solution.py:274
  612.7 687.0 %reduce-scatter.23.cloned.1.call-start = ((), (), s32[]{:S(2)}) async-start(), calls=%async_computation.23 | async-start | bytes 18874368 | tf_op jit(solution)/shard_map/reduce_scatter | solution.py:276
  630.0 0.7 copy-start.22
  630.1 0.8 copy-start.21
  630.1 0.8 copy-start.23
  630.1 58.9 %copy-start.5 = (bf16[1,256,2048]{2,1,0:T(8,128)(2,1)S(1)}, bf16[1,256,2048]{2,1,0:T(8,128)(2,1)}, u32[]{:S(2)}) copy-start(bf16[1,256,2048]{2,1,0:T(8,128)(2,1)} %param.20) | copy-start | bytes 3145732
  630.1 58.9 %copy-start.16 = (f32[2048]{0:T(1024)S(1)}, f32[2048]{0:T(1024)}, u32[]{:S(2)}) copy-start(f32[2048]{0:T(1024)} %param.23) | copy-start | bytes 24580
  630.1 58.9 %copy-start.18 = (f32[256]{0:T(256)S(1)}, f32[256]{0:T(256)}, u32[]{:S(2)}) copy-start(f32[256]{0:T(256)} %copy-done.17) | copy-start | bytes 3076
  630.1 58.9 %copy-start.20 = (f32[256]{0:T(256)S(1)}, f32[256]{0:T(256)}, u32[]{:S(2)}) copy-start(f32[256]{0:T(256)} %copy-done.19) | copy-start | bytes 3076
  630.1 207.3 %copy-start.24 = (f32[2048]{0:T(1024)S(1)}, f32[2048]{0:T(1024)}, u32[]{:S(2)}) copy-start(f32[2048]{0:T(1024)} %param.35) | copy-start | bytes 24580
  689.0 148.3 %copy-start.6 = (f32[1,256,2048]{2,1,0:T(8,128)S(1)}, f32[1,256,2048]{2,1,0:T(8,128)}, u32[]{:S(2)}) copy-start(f32[1,256,2048]{2,1,0:T(8,128)} %reduce-scatter.11.cloned.1.call-done) | copy-start | bytes 6291460
Sparse Core Ops, SparseCore 0:
  9.9 30.5 all-gather.10
  42.7 80.7 all-gather.8
  125.4 26.4 all-gather.12
  153.6 27.8 all-gather.14
  183.2 28.1 all-gather.16
  212.9 80.7 all-gather.22
  295.6 52.9 all-gather.18
  350.4 55.9 all-gather.20
  545.6 143.4 reduce-scatter.10
  691.2 146.1 reduce-scatter.8
  841.3 52.1 reduce-scatter.12
  897.6 51.3 reduce-scatter.14
  952.9 51.2 reduce-scatter.16
  1008.4 51.2 reduce-scatter.18
  1063.7 115.9 reduce-scatter.20
  1183.7 115.9 reduce-scatter.22
where the time goes:
time: 1320 us; the launch traced here: 1310 us
  waiting for transfers between devices  811 us (61%)
  matrix products  276 us (21%)
  blocking collectives  70.6 us (5%)
  other arithmetic  65.2 us (5%)
  local copies, waits for them, and re-layouts  60.1 us (5%)
  between operations  14.8 us (1%)
    reduce_scatter x1, waiting for transfers between devices, on_device(): lax.psum_scatter(fc1_weight_grad, 'dp', scatter_dimension=0, tiled=True)  120 us
    reduce_scatter x1, waiting for transfers between devices, on_device(): lax.psum_scatter(fc2_weight_grad, 'dp', scatter_dimension=1, tiled=True)  120 us
    reduce_scatter x1, waiting for transfers between devices, on_device(): lax.psum_scatter(partial_value.reshape(row_count, length, width), 'branch...  99.7 us
    all_gather x1, waiting for transfers between devices, on_device(): hidden = lax.all_gather(shard_hidden, 'branch', axis=1, tiled=True)  82.9 us
    all_gather x1, waiting for transfers between devices, on_device(): lax.all_gather(out_cotangent, 'branch', axis=1, tiled=True)  71 us
    dot_general x6, matrix products, times_transpose(): lax.dot_general(left, right, (((1,), (1,)), ((), ())), preferred_element_...  64.6 us
    dot_general x6, matrix products, contract_rows(): lax.dot_general(left, right, (((0,), (0,)), ((), ())), preferred_element_...  59.1 us
    reduce_scatter x1, waiting for transfers between devices, on_device(): lax.psum_scatter(key_weight_grad, 'dp', scatter_dimension=0, tiled=True)  55.5 us
  transfers between devices with their start and end apart: 16, of which 13 were waited for; matrix products, arithmetic and copies ran while one was open for 27% of the time, Pallas kernels for 0%

commit v1 on v0

v1 whole, which is shorter than its diff:
```python
import functools

import jax
import jax.numpy as jnp
from jax import lax
from jax.experimental import pallas as pl
from jax.experimental.pallas import tpu as pltpu
from jax.sharding import PartitionSpec as P

HEAD_DIM = 64
ROT = 32
EPSILON = 1e-05
NEGATIVE = -1e30
LANES = 128
TILE = 512
QBLOCK = 256
MESH = pl.DeviceIdType.MESH
BF16 = jnp.bfloat16
F32 = jnp.float32
GELU_C = 0.7978845608028654
GELU_A = 0.044715


def flip(index, bits):
    out = index
    bit = 1
    while bit <= bits:
        if bits & bit:
            out = out + bit * (1 - 2 * lax.rem(lax.div(index, bit), 2))
        bit *= 2
    return out


def dot_nn(left, right):
    return jnp.dot(left, right, preferred_element_type=F32)


def dot_nt(left, right):
    return lax.dot_general(left, right, (((1,), (1,)), ((), ())), preferred_element_type=F32)


def tile_of(extent, most=TILE):
    return min(most, extent)


def aligned(index, step):
    return pl.ds(pl.multiple_of(index * step, step), step)


class Chain:
    def __init__(self, own_src, buf, rows, count, sems, dp):
        self.own_src, self.buf, self.rows, self.count = own_src, buf, rows, count
        self.sems, self.dp = sems, dp
        self.z = lax.axis_index("branch")

    def block(self, slot):
        return self.buf.at[aligned(slot, self.rows), :]

    def copy(self, up, step, slot, src=None):
        send, recv = self.sems[0 if up else 2], self.sems[1 if up else 3]
        return pltpu.make_async_remote_copy(
            src_ref=self.block(slot) if src is None else src,
            dst_ref=self.block(slot),
            send_sem=send.at[step],
            recv_sem=recv.at[step],
            device_id=(self.dp, self.z + 1 if up else self.z - 1),
            device_id_type=MESH,
        )

    def sends(self, up, step):
        z, last = self.z, self.count - 1
        if up:
            return jnp.logical_and(z >= step, z < last)
        return jnp.logical_and(z + step <= last, z > 0)

    def receives(self, up, step):
        z, last = self.z, self.count - 1
        return z - 1 - step >= 0 if up else z + 1 + step <= last

    def sent_slot(self, up, step):
        return self.z - step if up else self.z + step

    def start(self):
        for up in (False, True):

            @pl.when(self.sends(up, 0))
            def _(up=up):
                self.copy(up, 0, self.z, self.own_src).start()

    def pump(self, step):
        for up in (False, True):

            @pl.when(self.sends(up, step))
            def _(up=up):
                slot = self.sent_slot(up, step)
                self.copy(up, step - 1, slot).wait_recv()
                self.copy(up, step, slot).start()

    def arrive(self):
        for step in range(self.count - 1):
            for up in (False, True):

                @pl.when(jnp.logical_and(self.receives(up, step), jnp.logical_not(self.sends(up, step + 1))))
                def _(up=up, step=step):
                    slot = self.z - 1 - step if up else self.z + 1 + step
                    self.copy(up, step, slot).wait_recv()

    def finish(self):
        for step in range(self.count - 1):
            for up in (False, True):

                @pl.when(self.sends(up, step))
                def _(up=up, step=step):
                    self.copy(up, step, self.sent_slot(up, step), self.own_src if step == 0 else None).wait_send()


class Gather:
    def __init__(self, index, shard, full, by_rows, chips, sems):
        self.index, self.shard, self.full, self.by_rows, self.chips = index, shard, full, by_rows, chips
        self.send, self.recv, self.pair_send, self.pair_recv, self.own = sems
        dp = lax.axis_index("dp")
        self.z = lax.axis_index("branch")
        self.core = lax.rem(dp, 2)
        self.chip = lax.div(dp, 2)
        self.width = shard.shape[0 if by_rows else 1]

    def slot(self, dp):
        part = aligned(dp, self.width)
        return self.full.at[part, :] if self.by_rows else self.full.at[:, part]

    def at(self, r, core):
        return flip(self.chip, r) * 2 + core

    def to_chip(self, r, landing):
        return pltpu.make_async_remote_copy(
            src_ref=self.shard,
            dst_ref=self.slot(landing),
            send_sem=self.send.at[self.index, r - 1],
            recv_sem=self.recv.at[self.index, r - 1],
            device_id=(self.at(r, self.core), self.z),
            device_id_type=MESH,
        )

    def to_pair(self, r, landing):
        return pltpu.make_async_remote_copy(
            src_ref=self.shard if r == 0 else self.slot(self.at(r, self.core)),
            dst_ref=self.slot(landing),
            send_sem=self.pair_send.at[self.index, r],
            recv_sem=self.pair_recv.at[self.index, r],
            device_id=(self.chip * 2 + 1 - self.core, self.z),
            device_id_type=MESH,
        )

    def keep(self):
        return pltpu.make_async_copy(self.shard, self.slot(self.at(0, self.core)), self.own.at[self.index])

    def start(self):
        for r in range(1, self.chips):
            self.to_chip(r, self.at(0, self.core)).start()

    def start_pair(self):
        self.to_pair(0, self.at(0, self.core)).start()
        self.keep().start()

    def pump(self, r):
        self.to_chip(r, self.at(r, self.core)).wait_recv()
        self.to_pair(r, self.at(r, self.core)).start()

    def arrive(self):
        self.keep().wait()
        for r in range(self.chips):
            self.to_pair(r, self.at(r, 1 - self.core)).wait_recv()

    def finish(self):
        for r in range(1, self.chips):
            self.to_chip(r, self.at(0, self.core)).wait_send()
        for r in range(self.chips):
            self.to_pair(r, self.at(r, self.core)).wait_send()


def greet(chips, count):
    dp, z = lax.axis_index("dp"), lax.axis_index("branch")
    core, chip = lax.rem(dp, 2), lax.div(dp, 2)
    barrier = pltpu.get_barrier_semaphore()
    for r in range(1, chips):
        pl.semaphore_signal(barrier, inc=1, device_id=(flip(chip, r) * 2 + core, z), device_id_type=MESH)
    pl.semaphore_signal(barrier, inc=1, device_id=(chip * 2 + 1 - core, z), device_id_type=MESH)
    for shift in (1, count - 1):
        pl.semaphore_signal(barrier, inc=1, device_id=(dp, lax.rem(z + shift, count)), device_id_type=MESH)
    pl.semaphore_wait(barrier, chips + 2)


def forward_kernel(
    chips, count,
    x, gain, beta, wqkv, wf1, wo, wf2, cot, bqkv, bf1, table_c, table_l, table_r, seg_col, seg_row,
    gqkv, gf1, go, gf2, gcot, hid_t, q_out, k_out, v_out, att_t_out, lse_out, act_t, dgelu, part_out,
    hid, vqkv, vf1, vf2, vo, q, k, v, att, att_t, lse, act, part, stage_a, stage_b,
    w_send, w_recv, p_send, p_recv, own_sem, h_us, h_ur, h_ds, h_dr, c_us, c_ur, c_ds, c_dr, load_sem, save_sem, st_sem,
):
    z = lax.axis_index("branch")
    dp = lax.axis_index("dp")
    rows, width = x.shape
    length = rows * count
    hcols = wo.shape[0]
    units = wf2.shape[0]
    sems = (w_send, w_recv, p_send, p_recv, own_sem)
    g_qkv = Gather(0, wqkv, gqkv, True, chips, sems)
    g_f1 = Gather(1, wf1, gf1, True, chips, sems)
    g_o = Gather(2, wo, go, False, chips, sems)
    g_f2 = Gather(3, wf2, gf2, False, chips, sems)
    own_rows = hid.at[aligned(z, rows), :]
    h_chain = Chain(own_rows, hid, rows, count, (h_us, h_ur, h_ds, h_dr), dp)
    c_chain = Chain(cot, gcot, rows, count, (c_us, c_ur, c_ds, c_dr), dp)

    greet(chips, count)
    for g in (g_qkv, g_f1, g_o, g_f2):
        g.start()
        g.start_pair()
    keep_cot = pltpu.make_async_copy(cot, gcot.at[aligned(z, rows), :], load_sem.at[5])
    keep_cot.start()

    step_rows = 32

    def norm(i, _):
        part_rows = aligned(i, step_rows)
        inputs = x[part_rows, :].astype(F32)
        center = inputs - jnp.mean(inputs, axis=-1, keepdims=True)
        inverse = lax.rsqrt(jnp.mean(center * center, axis=-1, keepdims=True) + EPSILON)
        where = pl.ds(pl.multiple_of(z * rows + i * step_rows, step_rows), step_rows)
        hid[where, :] = (center * inverse * gain[...] + beta[...]).astype(BF16)
        return 0

    lax.fori_loop(0, rows // step_rows, norm, 0)
    h_chain.start()
    for r in range(1, chips - 1):
        g_qkv.pump(r)
    if count > 2:
        h_chain.pump(1)
    if chips > 1:
        g_qkv.pump(chips - 1)
    g_qkv.arrive()
    load_qkv = pltpu.make_async_copy(gqkv, vqkv, load_sem.at[0])
    load_qkv.start()
    for s in range(2, count - 1):
        h_chain.pump(s)
    c_chain.start()
    h_chain.arrive()
    load_qkv.wait()

    mt = tile_of(length)
    ht = tile_of(hcols)

    def project(i, _):
        rows_i = aligned(i, mt)
        for which, dest in ((0, q), (1, k), (2, v)):
            for c in range(hcols // ht):
                at = which * hcols + c * ht
                y = dot_nn(hid[rows_i, :], vqkv[:, at : at + ht]) + bqkv[:, at : at + ht]
                for piece in range(ht // LANES):
                    part_y = y[:, piece * LANES : (piece + 1) * LANES]
                    to = c * ht + piece * LANES
                    if which < 2:
                        part_y = (
                            part_y * table_c[rows_i, :]
                            + pltpu.roll(part_y, LANES - ROT // 2, 1) * table_l[rows_i, :]
                            + pltpu.roll(part_y, ROT // 2, 1) * table_r[rows_i, :]
                        )
                    low = part_y.astype(BF16)
                    if which == 0:
                        low = low * BF16(HEAD_DIM**-0.5)
                    dest[rows_i, to : to + LANES] = low
        return 0

    lax.fori_loop(0, length // mt, project, 0)
    saves = []

    def save(src, dst):
        c = pltpu.make_async_copy(src, dst, save_sem.at[len(saves)])
        c.start()
        saves.append(c)

    save(q, q_out)
    save(k, k_out)
    save(v, v_out)
    if count > 2:
        c_chain.pump(1)

    qb = tile_of(length, QBLOCK)

    def attend(pair, _):
        cols = aligned(pair, LANES)
        lane = lax.broadcasted_iota(jnp.int32, (1, LANES), 1)
        for b in range(length // qb):
            here = slice(b * qb, (b + 1) * qb)
            before = b * qb
            q2 = q[here, cols]
            seg_q = seg_col[here, :]
            ki = lax.broadcasted_iota(jnp.int32, (qb, qb), 1)
            qi = lax.broadcasted_iota(jnp.int32, (qb, qb), 0)
            seen_here = jnp.logical_or(
                jnp.logical_and(seg_q == seg_row[:, here], ki <= qi), ki == qi
            )
            out = jnp.zeros((qb, LANES), F32)
            stat = jnp.zeros((qb, LANES), F32)
            for h in range(2):
                mine = (lane // HEAD_DIM) == h
                qh = jnp.where(mine, q2, BF16(0))
                s_here = jnp.where(seen_here, dot_nt(qh, k[here, cols]), NEGATIVE)
                top = jnp.max(s_here, axis=-1, keepdims=True)
                if before:
                    s_before = jnp.where(
                        seg_q == seg_row[:, :before], dot_nt(qh, k[:before, cols]), NEGATIVE
                    )
                    top = jnp.maximum(top, jnp.max(s_before, axis=-1, keepdims=True))
                e_here = jnp.exp(s_here - top)
                total = jnp.sum(e_here, axis=-1, keepdims=True)
                if before:
                    e_before = jnp.exp(s_before - top)
                    total = total + jnp.sum(e_before, axis=-1, keepdims=True)
                share = 1.0 / total
                o = dot_nn((e_here * share).astype(BF16), jnp.where(mine, v[here, cols], BF16(0)))
                if before:
                    o = o + dot_nn(
                        (e_before * share).astype(BF16), jnp.where(mine, v[:before, cols], BF16(0))
                    )
                out = out + o
                stat = jnp.where(mine, top + jnp.log(total), stat)
            att[here, cols] = out.astype(BF16)
            att_t[cols, here] = out.T.astype(BF16)
            turned = stat.T
            lse[pl.ds(2 * pair, 1), here] = turned[0:1, :]
            lse[pl.ds(2 * pair + 1, 1), here] = turned[HEAD_DIM : HEAD_DIM + 1, :]
        return 0

    pairs = hcols // LANES
    lax.fori_loop(0, pairs // 2, attend, 0)
    for r in range(1, chips):
        g_f1.pump(r)
    g_f1.arrive()
    load_f1 = pltpu.make_async_copy(gf1, vf1, load_sem.at[1])
    load_f1.start()
    for s in range(2, count - 1):
        c_chain.pump(s)
    lax.fori_loop(pairs // 2, pairs, attend, 0)
    save(att_t, att_t_out)
    save(lse, lse_out)
    for r in range(1, chips):
        g_o.pump(r)
    g_o.arrive()
    load_o = pltpu.make_async_copy(go, vo, load_sem.at[2])
    load_o.start()
    load_f1.wait()

    ft = tile_of(units)
    per_row = units // ft
    n_tiles = (length // mt) * per_row

    def staged(slot, rows_i, cols_i, which):
        src = (stage_a if which == 0 else stage_b).at[slot]
        dst = act_t.at[cols_i, rows_i] if which == 0 else dgelu.at[rows_i, cols_i]
        return pltpu.make_async_copy(src, dst, st_sem.at[which, slot])

    def unit(i, _):
        rows_i, cols_i = aligned(lax.div(i, per_row), mt), aligned(lax.rem(i, per_row), ft)
        slot = lax.rem(i, 2)

        @pl.when(i >= 2)
        def _():
            for which in range(2):
                staged(slot, rows_i, cols_i, which).wait()

        y = dot_nn(hid[rows_i, :], vf1[:, cols_i]) + bf1[:, cols_i]
        square = y * y
        t = jnp.tanh(GELU_C * (y + GELU_A * (y * square)))
        half = 0.5 * (1.0 + t)
        low = (y * half).astype(BF16)
        act[rows_i, cols_i] = low
        stage_a[slot] = low.T
        stage_b[slot] = (
            half + 0.5 * y * (1.0 - t * t) * (GELU_C * (1.0 + 3.0 * GELU_A * square))
        ).astype(BF16)
        for which in range(2):
            staged(slot, rows_i, cols_i, which).start()
        return 0

    lax.fori_loop(0, n_tiles, unit, 0)
    for i in range(max(n_tiles - 2, 0), n_tiles):
        for which in range(2):
            staged(i % 2, pl.ds(0, mt), pl.ds(0, ft), which).wait()

    wt = tile_of(width)
    per_col = width // wt
    n_turn = (length // mt) * per_col

    def turn_copy(slot, rows_i, cols_i):
        return pltpu.make_async_copy(
            stage_a.at[slot, pl.ds(0, wt), :], hid_t.at[cols_i, rows_i], st_sem.at[0, slot]
        )

    def turn(i, _):
        rows_i, cols_i = aligned(lax.div(i, per_col), mt), aligned(lax.rem(i, per_col), wt)
        slot = lax.rem(i, 2)

        @pl.when(i >= 2)
        def _():
            turn_copy(slot, rows_i, cols_i).wait()

        stage_a[slot, 0:wt, :] = hid[rows_i, cols_i].T
        turn_copy(slot, rows_i, cols_i).start()
        return 0

    lax.fori_loop(0, n_turn, turn, 0)
    for i in range(max(n_turn - 2, 0), n_turn):
        turn_copy(i % 2, pl.ds(0, mt), pl.ds(0, wt)).wait()

    for r in range(1, chips):
        g_f2.pump(r)
    g_f2.arrive()
    load_f2 = pltpu.make_async_copy(gf2, vf2, load_sem.at[3])
    load_f2.start()
    load_o.wait()
    load_f2.wait()

    def output(i, _):
        rows_i, cols_i = aligned(lax.div(i, per_col), mt), aligned(lax.rem(i, per_col), wt)
        part[rows_i, cols_i] = (
            dot_nn(act[rows_i, :], vf2[:, cols_i]) + dot_nn(att[rows_i, :], vo[:, cols_i])
        ).astype(BF16)
        return 0

    lax.fori_loop(0, n_turn, output, 0)
    save(part, part_out)
    c_chain.arrive()
    keep_cot.wait()
    for g in (g_qkv, g_f1, g_o, g_f2):
        g.finish()
    h_chain.finish()
    c_chain.finish()
    for c in saves:
        c.wait()


def run_forward(ndp, count, x, gain, beta, wqkv, wf1, wo, wf2, cot, bqkv, bf1, tables, seg_col, seg_row):
    chips = ndp // 2
    rows, width = x.shape
    length = rows * count
    hcols, units = wo.shape[0], wf2.shape[0]
    heads = hcols // HEAD_DIM
    mt, ft, wt = tile_of(length), tile_of(units), tile_of(width)
    anywhere = pl.BlockSpec(memory_space=pl.ANY)
    vmem = pl.BlockSpec(memory_space=pltpu.VMEM)
    low = lambda *shape: jax.ShapeDtypeStruct(shape, BF16)
    outs = [
        low(width, 3 * hcols), low(width, units), low(hcols, width), low(units, width), low(length, width),
        low(width, length), low(length, hcols), low(length, hcols), low(length, hcols), low(hcols, length),
        jax.ShapeDtypeStruct((heads, length), F32), low(units, length), low(length, units), low(length, width),
    ]
    v = lambda *shape: pltpu.VMEM(shape, BF16)
    steps = max(count - 1, 1)
    dma = lambda *shape: pltpu.SemaphoreType.DMA(shape)
    scratch = [
        v(length, width), v(width, 3 * hcols), v(width, units), v(units, width), v(hcols, width),
        v(length, hcols), v(length, hcols), v(length, hcols), v(length, hcols), v(hcols, length),
        pltpu.VMEM((heads, length), F32), v(length, units), v(length, width),
        v(2, max(ft, wt), mt), v(2, mt, ft),
        dma(4, max(chips - 1, 1)), dma(4, max(chips - 1, 1)), dma(4, chips), dma(4, chips), dma(4),
        *[dma(steps) for _ in range(8)], dma(6), dma(8), dma(2, 2),
    ]
    return pl.pallas_call(
        functools.partial(forward_kernel, chips, count),
        out_shape=outs,
        in_specs=[vmem, vmem, vmem, anywhere, anywhere, anywhere, anywhere, anywhere] + [vmem] * 7,
        out_specs=[anywhere] * len(outs),
        scratch_shapes=scratch,
        compiler_params=pltpu.CompilerParams(
            collective_id=0, has_side_effects=True, vmem_limit_bytes=60 * 1024 * 1024
        ),
        name="gather_forward",
    )(x, gain, beta, wqkv, wf1, wo, wf2, cot, bqkv, bf1, *tables, seg_col, seg_row)


def rotary_tables(segments):
    length = segments.shape[0]
    places = jnp.arange(length, dtype=jnp.int32)
    starts = jnp.zeros((length,), jnp.int32)
    for value in range(4):
        first = jnp.min(jnp.where(segments == value, places, length))
        starts = jnp.where(segments == value, first, starts)
    half_rot = ROT // 2
    frequency = 10000.0 ** (-2.0 * jnp.arange(half_rot, dtype=F32) / ROT)
    angles = (places - starts).astype(F32)[:, None] * frequency
    cosine, sine = jnp.cos(angles), jnp.sin(angles)
    one = jnp.ones((length, HEAD_DIM - ROT), F32)
    zero = jnp.zeros((length, HEAD_DIM - ROT), F32)
    none = jnp.zeros_like(sine)
    twice = lambda t: jnp.concatenate([t, t], axis=1)
    return (
        twice(jnp.concatenate([cosine, cosine, one], axis=1)),
        twice(jnp.concatenate([-sine, none, zero], axis=1)),
        twice(jnp.concatenate([none, sine, zero], axis=1)),
    ), cosine, sine


def contract_rows(left, right):
    return lax.dot_general(left, right, (((0,), (0,)), ((), ())), preferred_element_type=F32)


def rotate_back(tensor, cosine, sine):
    half_rot = ROT // 2
    lower_part = tensor[..., :half_rot]
    upper_part = tensor[..., half_rot:ROT]
    return jnp.concatenate(
        [
            lower_part * cosine + upper_part * sine,
            upper_part * cosine - lower_part * sine,
            tensor[..., ROT:],
        ],
        axis=-1,
    )


def attend_back(q, k, v, out_grad, lse, seg):
    length = q.shape[0]
    heads = q.shape[1] // HEAD_DIM
    split = lambda t: t.reshape(length, heads, HEAD_DIM)
    q, k, v, g = split(q), split(k), split(v), split(out_grad)
    places = jnp.arange(length)
    seen = (seg[:, None] == seg[None, :]) & (places[None, :] <= places[:, None]) & (seg[None, :] != 0)
    seen = seen | (places[None, :] == places[:, None])

    def one(member):
        qh, kh, vh, gh, lh = member
        s = jnp.where(seen, dot_nt(qh, kh), NEGATIVE)
        p = jnp.exp(s - lh[:, None])
        pg = dot_nt(gh, vh)
        delta = jnp.sum(p * pg, axis=-1, keepdims=True)
        sg = (p * (pg - delta)).astype(BF16)
        return (
            dot_nn(sg, kh) * HEAD_DIM**-0.5,
            contract_rows(sg, qh),
            contract_rows(p.astype(BF16), gh),
        )

    t = lambda a: a.transpose(1, 0, 2)
    dq, dk, dv = lax.map(one, (t(q), t(k), t(v), t(g), lse))
    return t(dq), t(dk), t(dv)


def on_device(
    ndp, count,
    block_input, segment_ids, out_cotangent, norm_gain, norm_bias, query_weight, key_weight, value_weight,
    query_bias, key_bias, value_bias, out_weight, fc1_weight, fc1_bias, fc2_weight, output_bias,
):
    x = block_input[0]
    cot = out_cotangent[0]
    seg = segment_ids[0]
    rows, width = x.shape
    length = rows * count
    tables, cosine, sine = rotary_tables(seg)
    wqkv = jnp.concatenate([query_weight, key_weight, value_weight], axis=1)
    bqkv = jnp.concatenate([query_bias, key_bias, value_bias])[None, :]
    hidden_seg = jnp.where(seg == 0, -1, seg)
    (gqkv, gf1, go, gf2, gcot, hid_t, q, k, v, att_t, lse, act_t, dgelu, part) = run_forward(
        ndp, count, x, norm_gain[None, :], norm_bias[None, :], wqkv, fc1_weight, out_weight, fc2_weight, cot,
        bqkv, fc1_bias[None, :], tables, seg[:, None], hidden_seg[None, :],
    )
    hcols = att_t.shape[0]
    inputs = x.astype(F32)
    center = inputs - jnp.mean(inputs, axis=-1, keepdims=True)
    inverse = lax.rsqrt(jnp.mean(center * center, axis=-1, keepdims=True) + EPSILON)
    normed = center * inverse
    summed = lax.psum_scatter(part, "branch", scatter_dimension=0, tiled=True).astype(F32)
    block_output = (inputs + summed + output_bias).astype(BF16)
    output_bias_grad = jnp.sum(gcot, axis=0, dtype=F32)
    out_weight_grad = dot_nn(att_t, gcot)
    fc2_weight_grad = dot_nn(act_t, gcot)
    pre_grad = (dot_nt(gcot, gf2) * dgelu.astype(F32)).astype(BF16)
    fc1_weight_grad = dot_nn(hid_t, pre_grad)
    fc1_bias_grad = jnp.sum(pre_grad, axis=0, dtype=F32)
    att_grad = dot_nt(gcot, go).astype(BF16)
    dq, dk, dv = attend_back(q, k, v, att_grad, lse, seg)
    cosine, sine = cosine[:, None, :], sine[:, None, :]
    flat = lambda t: t.astype(BF16).reshape(length, hcols)
    grads = jnp.concatenate(
        [flat(rotate_back(dq, cosine, sine)), flat(rotate_back(dk, cosine, sine)), flat(dv)], axis=1
    )
    qkv_weight_grad = dot_nn(hid_t, grads)
    qkv_bias_grad = jnp.sum(grads, axis=0, dtype=F32)
    hidden_grad = dot_nt(pre_grad, gf1) + dot_nt(grads, gqkv)
    norm_grad = lax.psum_scatter(hidden_grad.astype(BF16), "branch", scatter_dimension=0, tiled=True).astype(F32)
    gain_part = jnp.sum(norm_grad * normed, axis=0)
    beta_part = jnp.sum(norm_grad, axis=0)
    scaled = norm_grad * norm_gain
    input_grad = cot.astype(F32) + inverse * (
        scaled
        - jnp.mean(scaled, axis=-1, keepdims=True)
        - normed * jnp.mean(scaled * normed, axis=-1, keepdims=True)
    )
    gain_grad, norm_bias_grad = lax.psum((gain_part, beta_part), ("dp", "branch"))
    qkv_bias_grad, fc1_bias_grad, output_bias_grad = lax.psum(
        (qkv_bias_grad, fc1_bias_grad, output_bias_grad), "dp"
    )
    scatter = lambda g, dim: lax.psum_scatter(g.astype(BF16), "dp", scatter_dimension=dim, tiled=True).astype(F32)
    qkv_weight_grad = scatter(qkv_weight_grad, 0)
    fc1_weight_grad = scatter(fc1_weight_grad, 0)
    out_weight_grad = scatter(out_weight_grad, 1)
    fc2_weight_grad = scatter(fc2_weight_grad, 1)
    third = lambda t, i: t[..., i * hcols : (i + 1) * hcols]
    return (
        block_output[None], input_grad[None], gain_grad, norm_bias_grad,
        third(qkv_weight_grad, 0), third(qkv_weight_grad, 1), third(qkv_weight_grad, 2),
        third(qkv_bias_grad, 0), third(qkv_bias_grad, 1), third(qkv_bias_grad, 2),
        out_weight_grad, fc1_weight_grad, fc1_bias_grad, fc2_weight_grad, output_bias_grad,
    )


def solution(mesh):
    tokens, vector, split = P("dp", "branch", None), P(), P("branch")
    rows_first, cols_first = P("dp", "branch"), P("branch", "dp")
    in_specs = (
        tokens, P("dp", None), tokens, vector, vector, rows_first, rows_first, rows_first,
        split, split, split, cols_first, rows_first, split, cols_first, vector,
    )
    out_specs = (
        tokens, tokens, vector, vector, rows_first, rows_first, rows_first, split, split, split,
        cols_first, rows_first, split, cols_first, vector,
    )
    return jax.shard_map(
        functools.partial(on_device, mesh.shape["dp"], mesh.shape["branch"]),
        mesh=mesh, in_specs=in_specs, out_specs=out_specs, check_vma=False,
    )
```

time: 1320 us -> 718 us (0.54)
  waiting for transfers between devices: 811 us -> 242 us
  Pallas kernels: 0 us -> 165 us
  matrix products: 276 us -> 163 us
  local copies, waits for them, and re-layouts: 60.1 us -> 19.6 us
  other arithmetic: 65.2 us -> 37.6 us
    reduce_scatter x8 -> x6, waiting for transfers between devices: 588 us -> 241 us  [the longest x4 206 us: on_device(): lax.psum_scatter(g.astype(BF16), 'dp', scatter_dimension=dim, tiled=True)]
    all_gather x8 -> x0, waiting for transfers between devices: 219 us -> none  [the longest x1 82.9 us: on_device(): hidden = lax.all_gather(shard_hidden, 'branch', axis=1, tiled=True)]
    pallas_call x0 -> x1, Pallas kernels: none -> 165 us  [run_forward(): pl.pallas_call(functools.partial(forward_kernel, chips, count), out_shape...]
    dot_general x26 -> x32, matrix products: 217 us -> 140 us  [the longest x20 76.9 us: dot_nt(): lax.dot_general(left, right, (((1,), (1,)), ((), ())), preferred_element_...]
    dynamic_update_slice x6 -> x0, local copies, waits for them, and re-layouts: 43.4 us -> none  [attend_row(): lax.map(one_block, jnp.arange(length // block_rows, dtype=jnp.int32))]
    dot_general x6 -> x16, matrix products: 59.1 us -> 23.2 us  [contract_rows(): lax.dot_general(left, right, (((0,), (0,)), ((), ())), preferred_element_...]
    convert_element_type x4 -> x12, other arithmetic: 32.7 us -> 19 us  [the longest x8 9.1 us: one(): sg = (p * (pg - delta)).astype(BF16)]
  transfers between devices with their start and end apart: 16 -> 6, of which waited for: 13 -> 5; matrix products, arithmetic and copies ran while one was open for 27% -> 27% of each run, Pallas kernels for 0% -> 0%
where the time goes in v1:
time: 718 us; the launch traced here: 715 us
  waiting for transfers between devices  242 us (34%)
  Pallas kernels  165 us (23%)
  matrix products  163 us (23%)
  blocking collectives  72.4 us (10%)
  other arithmetic  37.6 us (5%)
  local copies, waits for them, and re-layouts  19.6 us (3%)
  between operations  14.7 us (2%)
    reduce_scatter x4, waiting for transfers between devices, on_device(): lax.psum_scatter(g.astype(BF16), 'dp', scatter_dimension=dim, tiled=True)  206 us
    pallas_call x1, Pallas kernels, run_forward(): pl.pallas_call(functools.partial(forward_kernel, chips, count), out_shape...  165 us
    dot_general x20, matrix products, dot_nt(): lax.dot_general(left, right, (((1,), (1,)), ((), ())), preferred_element_...  76.9 us
    dot_general x12, matrix products, dot_nn(): return jnp.dot(left, right, preferred_element_type=F32)  63 us
    psum x1, blocking collectives, on_device(): lax.psum((gain_part, beta_part), ('dp', 'branch'))  46.2 us
    reduce_scatter x1, waiting for transfers between devices, on_device(): lax.psum_scatter(part, 'branch', scatter_dimension=0, tiled=True)  32.1 us
    psum x1, blocking collectives, on_device(): lax.psum((qkv_bias_grad, fc1_bias_grad, output_bias_grad), 'dp')  26.2 us
    dot_general x16, matrix products, contract_rows(): lax.dot_general(left, right, (((0,), (0,)), ((), ())), preferred_element_...  23.2 us
  transfers between devices with their start and end apart: 6, of which 5 were waited for; matrix products, arithmetic and copies ran while one was open for 27% of the time, Pallas kernels for 0%

profile of v1, /device:TPU:0, one launch (start us, length us, event | category | flops | bytes accessed | tf_op | source)
XLA Modules:
  0.0 714.6 jit_solution(946457502449830256)
XLA Ops:
  11.2 2.6 subtract_convert_fusion.2
  13.8 1.9 multiply_sine_fusion
  15.8 1.9 concatenate.35.table_l
  17.8 1.7 concatenate.36.table_r
  20.6 1.7 concatenate.34.table_c
  23.3 165.1 %gather_forward.1 = (bf16[2048,1536]{1,0:T(8,128)(2,1)}, bf16[2048,2048]{1,0:T(8,128)(2,1)}, bf16[512,2048]{1,0:T(8,128)(2,1)}, bf16[2048,2048]{1,0:T(8,128)(2,1...) custom-call(bf16[256,2048]{1,0:T(8,128)(2,1)} %bitcast.118, ...), custom_call_target="tpu_custom_call" | custom-call | tf_op jit(solution)/shard_map/gather_forward/pallas_call | solution.py:469
  188.3 6.2 convolution_convert_fusion.3
  197.1 6.2 convolution_convert_fusion.4
  203.4 2.0 copy.51
  205.4 2.3 copy.52
  207.7 83.1 %while.15 = (s32[]{:T(128)}, f32[8,1024,64]{1,2,0:T(8,128)}, f32[8,1024,64]{1,2,0:T(8,128)}, bf16[8,1024,64]{1,2,0:T(8,128)(2,1)}, bf16[8,1024,64]{1,2,0:T(8,128...) while((s32[]{:T(128)}, f32[8,1024,64]{1,2,0:T(8,128)}, ...), condition=%wide.region_9.10_spmd.clone, body=%wide.region_7.9_spmd.clone.sunk | while | flops 685833216 | bytes 33458304 | solution.py:545
  207.7 1.7 fusion.92
  209.4 2.6 multiply_reduce_fusion.2
  213.1 2.1 fusion.93
  215.2 1.5 fusion.94
  218.1 1.7 fusion.92
  219.8 2.6 multiply_reduce_fusion.2
  223.5 2.1 fusion.93
  225.6 1.5 fusion.94
  228.5 1.7 fusion.92
  230.2 2.6 multiply_reduce_fusion.2
  233.9 2.1 fusion.93
  236.0 1.5 fusion.94
  238.9 1.7 fusion.92
  240.6 2.6 multiply_reduce_fusion.2
  244.3 2.1 fusion.93
  246.4 1.5 fusion.94
  249.3 1.7 fusion.92
  251.0 2.6 multiply_reduce_fusion.2
  254.7 2.1 fusion.93
  256.8 1.5 fusion.94
  259.7 1.7 fusion.92
  261.3 2.6 multiply_reduce_fusion.2
  265.1 2.1 fusion.93
  267.1 1.5 fusion.94
  270.0 1.7 fusion.92
  271.7 2.6 multiply_reduce_fusion.2
  275.4 2.1 fusion.93
  277.5 1.5 fusion.94
  280.4 1.7 fusion.92
  282.1 2.6 multiply_reduce_fusion.2
  285.8 2.1 fusion.93
  287.9 1.5 fusion.94
  293.5 13.3 %convert_reduce_fusion.1 = (f32[2048]{0:T(1024)S(1)}, bf16[1024,2048]{1,0:T(8,128)(2,1)S(1)}) fusion(bf16[1024,2048]{1,0:T(8,128)(2,1)} %get-tuple-element.86, bf16[1024,2048]{1,0:T(8,128)(2,1)} %get-tuple-element.84, bf16[2048,2048]{1,0:T(8,128)(2,1)} %get-tuple-element.85), kind=kOutput, calls=%fused_computation.40 | convolution fusion | flops 8600418304 | bytes 20979712 | tf_op jit(solution)/shard_map/dot_general | solution.py:39
  307.4 11.2 %fusion.55 = f32[1024,2048]{1,0:T(8,128)} fusion(bf16[1024,2048]{1,0:T(8,128)(2,1)S(1)} %get-tuple-element.213, bf16[2048,2048]{1,0:T(8,128)(2,1)S(1)} %bitcast.146), kind=kOutput, calls=%fused_computation.103 | convolution fusion | flops 8589934592 | bytes 20971520 | tf_op jit(solution)/shard_map/dot_general | solution.py:39
  318.7 12.4 %add_convert_fusion = bf16[1024,2048]{1,0:T(8,128)(2,1)} fusion(f32[1024,2048]{1,0:T(8,128)} %fusion.55, bf16[2048,1536]{1,0:T(8,128)(2,1)} %get-tuple-element.96, bf16[1024,512]{0,1:T(8,128)(2,1)S(1)} %bitcast.135, bf16[1024,512]{0,1:T(8,128)(2,1)S(1)} %bitcast.124, bf16[1024,512]{0,1:T(8,128)(2,1)S(1)} %bitcast.121), kind=kOutput, calls=%fused_computation.41 | convolution fusion | flops 6456082432 | bytes 22020096 | tf_op jit(solution)/shard_map/dot_general | solution.py:39
  331.9 11.8 %convolution_convert_fusion.2 = bf16[2048,1536]{1,0:T(8,128)(2,1)} fusion(bf16[2048,1024]{1,0:T(8,128)(2,1)} %get-tuple-element.97, bf16[1024,512]{0,1:T(8,128)(2,1)S(1)} %bitcast.136, bf16[1024,512]{0,1:T(8,128)(2,1)S(1)} %bitcast.125, bf16[1024,512]{0,1:T(8,128)(2,1)S(1)} %bitcast.122), kind=kOutput, calls=%fused_computation.45 | convolution fusion | flops 6455033856 | bytes 13631488 | tf_op jit(solution)/shard_map/dot_general | solution.py:35
  343.8 14.2 %convolution_convert_fusion.1 = bf16[2048,2048]{1,0:T(8,128)(2,1)} fusion(bf16[2048,1024]{1,0:T(8,128)(2,1)} %get-tuple-element.97, bf16[1024,2048]{1,0:T(8,128)(2,1)} %copy-done.13), kind=kOutput, calls=%fused_computation.44 | convolution fusion | flops 8594128896 | bytes 16777216 | tf_op jit(solution)/shard_map/dot_general | solution.py:35
  358.1 14.0 %convolution_convert_fusion = bf16[2048,2048]{1,0:T(8,128)(2,1)} fusion(bf16[2048,1024]{1,0:T(8,128)(2,1)} %get-tuple-element.99, bf16[1024,2048]{1,0:T(8,128)(2,1)} %get-tuple-element.84), kind=kOutput, calls=%fused_computation.43 | convolution fusion | flops 8594128896 | bytes 16777216 | tf_op jit(solution)/shard_map/dot_general | solution.py:35
  372.0 1.7 convert_reduce_fusion.2
  373.8 2.9 convert_reduce_fusion
  376.7 26.2 %all-reduce.1 = (f32[1536]{0:T(1024)S(1)}, f32[2048]{0:T(1024)}, f32[2048]{0:T(1024)}) all-reduce(f32[1536]{0:T(1024)S(1)} %convert_reduce_fusion.2, f32[2048]{0:T(1024)S(1)} %get-tuple-element.212, f32[2048]{0:T(1024)S(1)} %convert_reduce_fusion), channel_id=1, replica_groups=mesh['dp'=8,'branch'=4] {'dp'}, use_global_device_ids=true, to_apply=%region_19.20 | all-reduce | flops 5632 | bytes 45056 | tf_op jit(solution)/shard_map/psum | solution.py:600
  404.2 1.8 convert_element_type.107
  406.0 2.6 reduce-scatter.9.cloned.1.call-done
  408.6 2.3 fusion.50
  410.9 46.2 %all-reduce = (f32[2048]{0:T(1024)}, f32[2048]{0:T(1024)}) all-reduce(f32[2048]{0:T(1024)S(1)} %get-tuple-element.148, f32[2048]{0:T(1024)S(1)} %get-tuple-element.151), channel_id=1, replica_groups=mesh['dp'=8,'branch'=4] {'dp','branch'}, use_global_device_ids=true, to_apply=%region_14.15 | all-reduce | flops 4096 | bytes 32768 | tf_op jit(solution)/shard_map/psum | solution.py:599
  457.1 32.1 %reduce-scatter.7.cloned.1.call-done = bf16[256,2048]{1,0:T(8,128)(2,1)} async-done(((bf16[1024,2048]{1,0:T(8,128)(2,1)}), bf16[256,2048]{1,0:T(8,128)(2,1)}) %reduce-scatter.7.cloned.1.call-update) | async-done | bytes 1048592 | tf_op jit(solution)/shard_map/reduce_scatter | solution.py:572
  489.2 4.3 fusion.45
  493.6 61.6 %reduce-scatter.11.cloned.1.call-done = bf16[256,1536]{1,0:T(8,128)(2,1)} async-done(((bf16[2048,1536]{1,0:T(8,128)(2,1)}), bf16[256,1536]{1,0:T(8,128)(2,1)}) %reduce-scatter.11.cloned.1.call-update) | async-done | bytes 786448 | tf_op jit(solution)/shard_map/reduce_scatter | solution.py:603
  555.2 2.3 fusion.53
  557.5 72.3 %reduce-scatter.15.cloned.1.call-done = bf16[256,2048]{1,0:T(8,128)(2,1)} async-done(((bf16[2048,2048]{1,0:T(8,128)(2,1)}), bf16[256,2048]{1,0:T(8,128)(2,1)}) %reduce-scatter.15.cloned.1.call-update) | async-done | bytes 1048592 | tf_op jit(solution)/shard_map/reduce_scatter | solution.py:603
  629.8 2.8 convert_element_type.109
  632.5 72.2 %reduce-scatter.17.cloned.1.call-done = bf16[2048,256]{1,0:T(8,128)(2,1)} async-done(((bf16[2048,2048]{1,0:T(8,128)(2,1)}), bf16[2048,256]{1,0:T(8,128)(2,1)}) %reduce-scatter.17.cloned.1.call-update) | async-done | bytes 1048592 | tf_op jit(solution)/shard_map/reduce_scatter | solution.py:603
  704.8 2.7 convert_element_type.112
  (99 shorter events, 34.6 us)
Async XLA Ops:
  7.2 397.0 %reduce-scatter.13.cloned.1.call-start = ((), (), s32[]{:S(2)}) async-start(), calls=%async_computation.9 | async-start | bytes 2359296 | tf_op jit(solution)/shard_map/reduce_scatter | solution.py:603
  15.7 3.8 copy-start.11
  17.7 4.6 copy-start.7
  17.7 4.6 copy-start.8
  17.7 4.6 copy-start.9
  188.3 6.7 copy-start.6
  194.6 1.2 copy-start.5
  194.6 214.0 %reduce-scatter.9.cloned.1.call-start = ((), (), s32[]{:S(2)}) async-start(), calls=%async_computation.7 | async-start | bytes 5242880 | tf_op jit(solution)/shard_map/reduce_scatter | solution.py:590
  293.4 14.0 %slice-start = ((s8[8388608]{0:T(1024)(128)(4,1)}), s8[4194304]{0:T(1024)(128)(4,1)S(1)}, s32[]{:S(2)}) async-start(s8[8388608]{0:T(1024)(128)(4,1)} %bitcast.145), calls=%async_computation.12 | async-start | bytes 8388608
  293.4 13.4 %copy-start.2 = (f32[8,1024,64]{1,2,0:T(8,128)S(1)}, f32[8,1024,64]{1,2,0:T(8,128)}, u32[]{:S(2)}) copy-start(f32[8,1024,64]{1,2,0:T(8,128)} %get-tuple-element.93) | copy-start | bytes 6291460
  293.4 13.4 %copy-start.3 = (f32[8,1024,64]{1,2,0:T(8,128)S(1)}, f32[8,1024,64]{1,2,0:T(8,128)}, u32[]{:S(2)}) copy-start(f32[8,1024,64]{1,2,0:T(8,128)} %get-tuple-element.94) | copy-start | bytes 6291460
  293.5 13.9 %slice-start.1 = ((s8[8388608]{0:T(1024)(128)(4,1)}), s8[4194304]{0:T(1024)(128)(4,1)S(1)}, s32[]{:S(2)}) async-start(s8[8388608]{0:T(1024)(128)(4,1)} %bitcast.145), calls=%async_computation.13 | async-start | bytes 8388608
  306.8 11.8 %copy-start.13 = (bf16[1024,2048]{1,0:T(8,128)(2,1)}, bf16[1024,2048]{1,0:T(8,128)(2,1)S(1)}, u32[]{:S(2)}) copy-start(bf16[1024,2048]{1,0:T(8,128)(2,1)S(1)} %get-tuple-element.213) | copy-start | bytes 12582916
  307.4 11.2 %copy-start.4 = (bf16[8,1024,64]{1,2,0:T(8,128)(2,1)S(1)}, bf16[8,1024,64]{1,2,0:T(8,128)(2,1)}, u32[]{:S(2)}) copy-start(bf16[8,1024,64]{1,2,0:T(8,128)(2,1)} %get-tuple-element.95) | copy-start | bytes 3145732
  331.1 158.1 %reduce-scatter.7.cloned.1.call-start = ((), (), s32[]{:S(2)}) async-start(), calls=%async_computation.6 | async-start | bytes 5242880 | tf_op jit(solution)/shard_map/reduce_scatter | solution.py:572
  331.8 223.3 %reduce-scatter.11.cloned.1.call-start = ((), (), s32[]{:S(2)}) async-start(), calls=%async_computation.8 | async-start | bytes 7077888 | tf_op jit(solution)/shard_map/reduce_scatter | solution.py:603
  343.7 286.0 %reduce-scatter.15.cloned.1.call-start = ((), (), s32[]{:S(2)}) async-start(), calls=%async_computation.10 | async-start | bytes 9437184 | tf_op jit(solution)/shard_map/reduce_scatter | solution.py:603
  358.0 346.8 %reduce-scatter.17.cloned.1.call-start = ((), (), s32[]{:S(2)}) async-start(), calls=%async_computation.11 | async-start | bytes 9437184 | tf_op jit(solution)/shard_map/reduce_scatter | solution.py:603
  372.0 30.9 %copy-start = (bf16[1,256,2048]{2,1,0:T(8,128)(2,1)S(1)}, bf16[1,256,2048]{2,1,0:T(8,128)(2,1)}, u32[]{:S(2)}) copy-start(bf16[1,256,2048]{2,1,0:T(8,128)(2,1)} %param.18) | copy-start | bytes 3145732
  373.8 34.8 %copy-start.10 = (f32[2048]{0:T(1024)S(1)}, f32[2048]{0:T(1024)}, u32[]{:S(2)}) copy-start(f32[2048]{0:T(1024)} %param.21) | copy-start | bytes 24580
  373.8 115.4 %copy-start.1 = (bf16[1,256,2048]{2,1,0:T(8,128)(2,1)S(1)}, bf16[1,256,2048]{2,1,0:T(8,128)(2,1)}, u32[]{:S(2)}) copy-start(bf16[1,256,2048]{2,1,0:T(8,128)(2,1)} %param.20) | copy-start | bytes 3145732
  373.8 115.4 %copy-start.12 = (f32[2048]{0:T(1024)S(1)}, f32[2048]{0:T(1024)}, u32[]{:S(2)}) copy-start(f32[2048]{0:T(1024)} %param.33) | copy-start | bytes 24580
Sparse Core Ops, SparseCore 0:
  194.7 41.8 reduce-scatter.12
  331.2 77.3 reduce-scatter.8
  410.9 78.2 reduce-scatter.6
  492.8 62.2 reduce-scatter.10
  558.5 71.2 reduce-scatter.14
  633.5 71.2 reduce-scatter.16
